TPU v7x, 256 devices: a whole 4x4x8 slice. The times are simulated.
256 devices in a mesh: sp: 32 (over x, y, core), tp: 8 (over z).
Axes of the slice: x: 4, y: 4, z: 8, core: 2. Of those that a mesh axis runs over, the one named last changes fastest.
Arguments:
- queries: bfloat16 [16384, 8192], P('sp', 'tp'), may hold values from -200 to 200
- keys: bfloat16 [16384, 1024], P('sp', 'tp'), may hold values from -6 to 6
- values: bfloat16 [16384, 1024], P('sp', 'tp'), may hold values from -6 to 6
- w_out: bfloat16 [8192, 4096], P('tp'), may hold values from -0.0625 to 0.0625
- lengths: int32 [4], replicated, may hold values from 1 to 4096
- stretch_owner: int32 [32], replicated, may hold values from 0 to 31, as said below
- home_replica: int32 [4], replicated, may hold values from 0 to 31, as said below
Outputs:
- mixed: bfloat16 [16384, 4096], P(('sp', 'tp'))
- cache_keys: bfloat16 [131072, 1024], P('sp', 'tp')
- home_cache_values: bfloat16 [131072, 1024], P('sp', 'tp')
Inputs may be any that keep to these rules, and one draw needn't show every extreme that they name: Stretch c of prompt p stands on replica stretch_owner[p * 8 + c]; every replica appears once. `home_replica`: the prompts' home replicas are distinct; prompt 0's home is (stretch_owner[0] + 32 / 2) modulo 32.
All inputs are finite; a program needn't handle non-finite values.
Results may differ from a plain program's by a relative error of at most 0.014.
Values may be sent and summed in bfloat16 or wider, within the bound.
No kernel may reach another device: no remote copies, remote signals or barrier semaphores. Data moves between devices by JAX's collectives and lax.ppermute only.
A program may use at most 128 MiB of HBM per device.

v0:
```python
import math

import jax
import jax.numpy as jnp
from jax import lax
from jax.sharding import PartitionSpec as P

HEAD_DIM = 128
MAX_STRETCHES = 8


def sent_together(arrays, axis, dim, along):
    ends, at = ([], 0)
    for a in arrays[:-1]:
        at += a.shape[along]
        ends.append(at)
    both = jnp.concatenate(arrays, axis=along)
    return tuple(jnp.split(lax.all_gather(both, axis, axis=dim, tiled=True), ends, axis=along))


def lookup(table, position):
    entries = jnp.arange(table.shape[0], dtype=jnp.int32)
    return jnp.sum(jnp.where(position[..., None] == entries, table, 0), axis=-1)


def shards(queries, keys, values, w_out, lengths, stretch_owner, home_replica):
    stretch = queries.shape[0]
    width = keys.shape[1]
    local_kv = width // HEAD_DIM
    local_heads = queries.shape[1] // HEAD_DIM
    group_size = local_heads // local_kv
    score_scale = HEAD_DIM ** (-0.5)
    cache_span = MAX_STRETCHES * stretch
    replicas = lax.axis_size("sp")
    self_index = lax.axis_index("sp")
    owners = jnp.arange(replicas, dtype=jnp.int32)
    stretch_of = jnp.sum(
        jnp.where(stretch_owner[:, None] == owners[None, :], owners[:, None], 0), axis=0
    )
    my_stretch = lookup(stretch_of, jnp.asarray(self_index, jnp.int32))
    my_prompt = my_stretch // MAX_STRETCHES
    my_length = lookup(lengths, my_prompt)
    query_position = my_stretch % MAX_STRETCHES * stretch + jnp.arange(stretch, dtype=jnp.int32)
    live_rows = query_position < my_length
    query_head_rows = queries.reshape(stretch, local_kv, group_size, HEAD_DIM)

    def key_info(first_row, row_count):
        global_rows = first_row + jnp.arange(row_count, dtype=jnp.int32)
        key_stretch = lookup(stretch_of, global_rows // stretch)
        key_prompt = key_stretch // MAX_STRETCHES
        key_position = key_stretch % MAX_STRETCHES * stretch + global_rows % stretch
        key_live = key_position < lookup(lengths, key_prompt)
        return (key_prompt, key_position, key_live)

    def block_update(softmax_state, key_tile, value_block, first_row):
        row_count = key_tile.shape[0]
        key_prompt, key_position, key_live = key_info(first_row, row_count)
        visible = ((key_prompt == my_prompt) & key_live)[None, :] & (
            key_position[None, :] <= query_position[:, None]
        )

        def update_block(carried):
            running_max, totals, accum = carried
            key_portion = key_tile.reshape(row_count, local_kv, HEAD_DIM)
            value_split = value_block.reshape(row_count, local_kv, HEAD_DIM)
            scores = (
                jnp.einsum(
                    "cwxa,uwa->wxcu",
                    query_head_rows,
                    key_portion,
                    preferred_element_type=jnp.float32,
                )
                * score_scale
            )
            scores = jnp.where(visible, scores, -1e30)
            new_max = jnp.maximum(running_max, jnp.max(scores, axis=-1))
            weights = jnp.where(visible, jnp.exp(scores - new_max[..., None]), 0.0)
            rescale = jnp.exp(running_max - new_max)
            totals = rescale * totals + jnp.sum(weights, axis=-1)
            accum = rescale[..., None] * accum + jnp.einsum(
                "jfqm,mjy->jfqy",
                weights.astype(jnp.bfloat16),
                value_split,
                preferred_element_type=jnp.float32,
            )
            return (new_max, totals, accum)

        def unchanged(carried):
            return carried

        return lax.cond(jnp.any(visible), update_block, unchanged, softmax_state)

    start_state = (
        jnp.full((local_kv, group_size, stretch), -1e30, jnp.float32),
        jnp.zeros((local_kv, group_size, stretch), jnp.float32),
        jnp.zeros((local_kv, group_size, stretch, HEAD_DIM), jnp.float32),
    )
    empty_cache = jnp.zeros((cache_span, width), jnp.bfloat16)
    shard_piece = sent_together((keys, values), "sp", 0, 1)
    key_piece = shard_piece[0]
    value_piece = shard_piece[1]
    row_count = key_piece.shape[0]
    block_rows = math.gcd(row_count, 512)
    block_count = row_count // block_rows
    key_blocks = key_piece.reshape(block_count, block_rows, width)
    value_blocks = value_piece.reshape(block_count, block_rows, width)

    def step_block_update(carried, operands):
        key_tile, value_block, block_index = operands
        return (block_update(carried, key_tile, value_block, block_index * block_rows), None)

    result, unused = lax.scan(
        step_block_update,
        start_state,
        (key_blocks, value_blocks, jnp.arange(block_count, dtype=jnp.int32)),
    )
    shard_piece = sent_together((keys, values), "sp", 0, 1)
    key_piece = shard_piece[0]
    value_piece = shard_piece[1]
    row_count = key_piece.shape[0]
    place_block_rows = math.gcd(row_count, stretch)
    block_count = row_count // place_block_rows
    key_blocks = key_piece.reshape(block_count, place_block_rows, width)
    value_blocks = value_piece.reshape(block_count, place_block_rows, width)
    offsets = jnp.arange(place_block_rows, dtype=jnp.int32)

    def place_block(carried, operands):
        key_tile, value_tile, block_index = operands
        first = block_index * place_block_rows
        key_stretch = lookup(stretch_of, first // stretch)
        key_prompt = key_stretch // MAX_STRETCHES
        first_position = key_stretch % MAX_STRETCHES * stretch + first % stretch
        key_live = first_position + offsets < lookup(lengths, key_prompt)
        homed = lookup(home_replica, key_prompt) == self_index
        start = jnp.where(homed, first_position, 0)
        zero_column = jnp.zeros((), jnp.int32)
        results = []
        for buffer, tile in ((carried[0], key_tile), (carried[1], value_tile)):
            old = lax.dynamic_slice(buffer, (start, zero_column), (place_block_rows, width))
            kept = jnp.where(key_live[:, None], tile, jnp.zeros_like(tile))
            fresh = jnp.where(homed, kept, old)
            results.append(lax.dynamic_update_slice(buffer, fresh, (start, zero_column)))
        return ((results[0], results[1]), None)

    place_result, unused = lax.scan(
        place_block,
        (empty_cache, empty_cache),
        (key_blocks, value_blocks, jnp.arange(block_count, dtype=jnp.int32)),
    )
    running_max, totals, accum = result
    outputs = accum / totals[..., None]
    outputs = outputs.transpose(2, 0, 1, 3).reshape(stretch, local_heads * HEAD_DIM)
    attended = (outputs * live_rows[:, None].astype(jnp.float32)).astype(jnp.bfloat16)
    partial_sums = jnp.dot(attended, w_out, preferred_element_type=jnp.float32)
    mixed = lax.psum_scatter(
        partial_sums.astype(jnp.bfloat16), "tp", scatter_dimension=0, tiled=True
    )
    return (mixed, place_result[0], place_result[1])


def solution(mesh):
    placed = (P("sp", "tp"), P("sp", "tp"), P("sp", "tp"), P("tp", None), P(), P(), P())
    return jax.shard_map(
        shards,
        mesh=mesh,
        in_specs=placed,
        out_specs=(P(("sp", "tp"), None), P("sp", "tp"), P("sp", "tp")),
        check_vma=False,
    )
```

profile of v0, /device:TPU:3, one launch (start us, length us, event | category | flops | bytes accessed | tf_op | source)
XLA Modules:
  0.0 542.3 jit_solution(3066318422967128592)
XLA Ops:
  16.4 56.1 %all-gather.2.cloned.1.call-done = bf16[16384,256]{1,0:T(8,128)(2,1)} async-done(((bf16[512,256]{1,0:T(8,128)(2,1)}), bf16[16384,256]{1,0:T(8,128)(2,1)}) %all-gather.2.cloned.1.call-update) | async-done | bytes 8388624 | tf_op jit(solution)/shard_map/all_gather | solution.py:18
  72.5 5.7 %fusion.43 = (bf16[16384,128]{1,0:T(8,128)(2,1)}, bf16[16384,128]{1,0:T(8,128)(2,1)}) fusion(bf16[16384,256]{1,0:T(8,128)(2,1)} %all-gather.2.cloned.1.call-done), kind=kLoop, calls=%fused_computation.79 | loop fusion | bytes 16777216 | tf_op jit(solution)/shard_map/split | solution.py:18
  78.3 166.9 %while.34 = (s32[]{:T(128)}, f32[1,8,512]{2,1,0:T(8,128)S(1)}, f32[1,8,512]{2,1,0:T(8,128)S(1)}, f32[1,8,512,128]{3,2,1,0:T(8,128)S(1)}, s32[32]{0:T(128)S(1)}, ...) while((s32[]{:T(128)}, f32[1,8,512]{2,1,0:T(8,128)S(1)}, ...), condition=%wide.region_10.11_spmd.clone, body=%wide.region_2.10_spmd.clone.sunk | while | flops 1102941184 | bytes 32010684 | solution.py:112
  109.1 8.6 %conditional.3 = ((f32[1,8,512]{2,1,0:T(8,128)S(1)}, f32[1,8,512]{2,1,0:T(8,128)S(1)}, f32[1,8,512,128]{3,2,1,0:T(8,128)S(1)})) conditional(s32[]{:T(128)} %convert_element_type.40, (f32[1,8,512]{2,1,0:T(8,128)S(1)}, f32[1,8,512]{2,1,0:T(8,128)S(1)}, f32[1,8,512,128]{3,2,1,0:T(8,128)S(1)}) %tuple.95, (pred[512,512]{0,1:T(8,128)(4,1)S(1)}, ...), branch_computations={%region_6.6_spmd, %region_7.9_spmd} | conditional | flops 1102065664 | bytes 31720480 | solution.py:91
  109.1 2.4 fusion.4
  111.6 4.0 bitcast_add_fusion
  123.8 8.6 %conditional.3 = ((f32[1,8,512]{2,1,0:T(8,128)S(1)}, f32[1,8,512]{2,1,0:T(8,128)S(1)}, f32[1,8,512,128]{3,2,1,0:T(8,128)S(1)})) conditional(s32[]{:T(128)} %convert_element_type.40, (f32[1,8,512]{2,1,0:T(8,128)S(1)}, f32[1,8,512]{2,1,0:T(8,128)S(1)}, f32[1,8,512,128]{3,2,1,0:T(8,128)S(1)}) %tuple.95, (pred[512,512]{0,1:T(8,128)(4,1)S(1)}, ...), branch_computations={%region_6.6_spmd, %region_7.9_spmd} | conditional | flops 1102065664 | bytes 31720480 | solution.py:91
  126.3 4.0 bitcast_add_fusion
  144.7 8.6 %conditional.3 = ((f32[1,8,512]{2,1,0:T(8,128)S(1)}, f32[1,8,512]{2,1,0:T(8,128)S(1)}, f32[1,8,512,128]{3,2,1,0:T(8,128)S(1)})) conditional(s32[]{:T(128)} %convert_element_type.40, (f32[1,8,512]{2,1,0:T(8,128)S(1)}, f32[1,8,512]{2,1,0:T(8,128)S(1)}, f32[1,8,512,128]{3,2,1,0:T(8,128)S(1)}) %tuple.95, (pred[512,512]{0,1:T(8,128)(4,1)S(1)}, ...), branch_computations={%region_6.6_spmd, %region_7.9_spmd} | conditional | flops 1102065664 | bytes 31720480 | solution.py:91
  144.7 2.4 fusion.4
  147.1 4.0 bitcast_add_fusion
  156.3 8.6 %conditional.3 = ((f32[1,8,512]{2,1,0:T(8,128)S(1)}, f32[1,8,512]{2,1,0:T(8,128)S(1)}, f32[1,8,512,128]{3,2,1,0:T(8,128)S(1)})) conditional(s32[]{:T(128)} %convert_element_type.40, (f32[1,8,512]{2,1,0:T(8,128)S(1)}, f32[1,8,512]{2,1,0:T(8,128)S(1)}, f32[1,8,512,128]{3,2,1,0:T(8,128)S(1)}) %tuple.95, (pred[512,512]{0,1:T(8,128)(4,1)S(1)}, ...), branch_computations={%region_6.6_spmd, %region_7.9_spmd} | conditional | flops 1102065664 | bytes 31720480 | solution.py:91
  158.7 4.0 bitcast_add_fusion
  167.9 8.6 %conditional.3 = ((f32[1,8,512]{2,1,0:T(8,128)S(1)}, f32[1,8,512]{2,1,0:T(8,128)S(1)}, f32[1,8,512,128]{3,2,1,0:T(8,128)S(1)})) conditional(s32[]{:T(128)} %convert_element_type.40, (f32[1,8,512]{2,1,0:T(8,128)S(1)}, f32[1,8,512]{2,1,0:T(8,128)S(1)}, f32[1,8,512,128]{3,2,1,0:T(8,128)S(1)}) %tuple.95, (pred[512,512]{0,1:T(8,128)(4,1)S(1)}, ...), branch_computations={%region_6.6_spmd, %region_7.9_spmd} | conditional | flops 1102065664 | bytes 31720480 | solution.py:91
  170.4 4.0 bitcast_add_fusion
  188.8 8.6 %conditional.3 = ((f32[1,8,512]{2,1,0:T(8,128)S(1)}, f32[1,8,512]{2,1,0:T(8,128)S(1)}, f32[1,8,512,128]{3,2,1,0:T(8,128)S(1)})) conditional(s32[]{:T(128)} %convert_element_type.40, (f32[1,8,512]{2,1,0:T(8,128)S(1)}, f32[1,8,512]{2,1,0:T(8,128)S(1)}, f32[1,8,512,128]{3,2,1,0:T(8,128)S(1)}) %tuple.95, (pred[512,512]{0,1:T(8,128)(4,1)S(1)}, ...), branch_computations={%region_6.6_spmd, %region_7.9_spmd} | conditional | flops 1102065664 | bytes 31720480 | solution.py:91
  188.8 2.4 fusion.4
  191.2 4.0 bitcast_add_fusion
  215.8 8.6 %conditional.3 = ((f32[1,8,512]{2,1,0:T(8,128)S(1)}, f32[1,8,512]{2,1,0:T(8,128)S(1)}, f32[1,8,512,128]{3,2,1,0:T(8,128)S(1)})) conditional(s32[]{:T(128)} %convert_element_type.40, (f32[1,8,512]{2,1,0:T(8,128)S(1)}, f32[1,8,512]{2,1,0:T(8,128)S(1)}, f32[1,8,512,128]{3,2,1,0:T(8,128)S(1)}) %tuple.95, (pred[512,512]{0,1:T(8,128)(4,1)S(1)}, ...), branch_computations={%region_6.6_spmd, %region_7.9_spmd} | conditional | flops 1102065664 | bytes 31720480 | solution.py:91
  218.3 4.0 bitcast_add_fusion
  227.4 8.6 %conditional.3 = ((f32[1,8,512]{2,1,0:T(8,128)S(1)}, f32[1,8,512]{2,1,0:T(8,128)S(1)}, f32[1,8,512,128]{3,2,1,0:T(8,128)S(1)})) conditional(s32[]{:T(128)} %convert_element_type.40, (f32[1,8,512]{2,1,0:T(8,128)S(1)}, f32[1,8,512]{2,1,0:T(8,128)S(1)}, f32[1,8,512,128]{3,2,1,0:T(8,128)S(1)}) %tuple.95, (pred[512,512]{0,1:T(8,128)(4,1)S(1)}, ...), branch_computations={%region_6.6_spmd, %region_7.9_spmd} | conditional | flops 1102065664 | bytes 31720480 | solution.py:91
  229.9 4.0 bitcast_add_fusion
  249.3 9.5 %convolution_convert_fusion = bf16[512,4096]{1,0:T(8,128)(2,1)} fusion(bf16[512,1024]{0,1:T(8,128)(2,1)S(1)} %fusion.38, bf16[1024,4096]{1,0:T(8,128)(2,1)} %param.16), kind=kOutput, calls=%fused_computation.66 | convolution fusion | flops 4297064448 | bytes 13631488 | tf_op jit(solution)/shard_map/dot_general | solution.py:154
  259.4 274.7 %while.35 = (s32[]{:T(128)}, bf16[4096,128]{1,0:T(8,128)(2,1)S(1)}, bf16[4096,128]{1,0:T(8,128)(2,1)S(1)}, s32[32]{0:T(128)S(1)}, s32[32]{0:T(128)S(1)}, /*index...) while((s32[]{:T(128)}, bf16[4096,128]{1,0:T(8,128)(2,1)S(1)}, ...), condition=%wide.region_17.18_spmd.clone, body=%wide.region_13.17_spmd.clone.sunk | while | flops 263329 | bytes 1312616 | solution.py:145
  (571 shorter events, 243.3 us)
Async XLA Ops:
  7.2 8.0 %copy-start.2 = (s32[4]{0:T(128)S(1)}, s32[4]{0:T(128)}, u32[]{:S(2)}) copy-start(s32[4]{0:T(128)} %param.17) | copy-start | bytes 52
  7.2 65.3 %all-gather.2.cloned.1.call-start = ((), (), s32[]{:S(2)}) async-start(), calls=%async_computation.1 | async-start | bytes 8650752 | tf_op jit(solution)/shard_map/all_gather | solution.py:18
  8.9 525.2 %reduce-scatter.2.cloned.1.call-start = ((), (), s32[]{:S(2)}) async-start(), calls=%async_computation.2 | async-start | bytes 4718592 | tf_op jit(solution)/shard_map/reduce_scatter | solution.py:155
  258.8 0.7 copy-start.3
  534.1 1.0 copy-start
  534.1 1.3 copy-start.1
Sparse Core Ops, SparseCore 0:
  11.1 61.2 all-gather.1
  258.9 52.1 reduce-scatter.1
where the time goes:
time: 546 us; the launch traced here: 542 us
  loops' own time  172 us (32%)
  other arithmetic  157 us (29%)
  local copies, waits for them, and re-layouts  79.2 us (15%)
  matrix products  61 us (11%)
  waiting for transfers between devices  56.1 us (10%)
  between operations  16.8 us (3%)
    another operation x1, loops' own time, shards(): lax.scan(place_block, (empty_cache, empty_cache), (key_blocks, value_bloc...  128 us
    all_gather x1, waiting for transfers between devices, sent_together(): lax.all_gather(both, axis, axis=dim, tiled=True)  56.1 us
    reduce_sum x130, other arithmetic, lookup(): return jnp.sum(jnp.where(position[..., None] == entries, table, 0), axis=-1)  47.7 us
    another operation x1, loops' own time, shards(): lax.scan(step_block_update, start_state, (key_blocks, value_blocks, jnp.a...  43 us
    dynamic_slice x64, local copies, waits for them, and re-layouts, shards(): lax.scan(step_block_update, start_state, (key_blocks, value_blocks, jnp.a...  37.5 us
    select_n x32, other arithmetic, place_block(): fresh = jnp.where(homed, kept, old)  37.4 us
    dot_general x8, matrix products, update_block(): jnp.einsum('jfqm,mjy->jfqy', weights.astype(jnp.bfloat16), value_split, p...  32.3 us
    dynamic_update_slice x64, local copies, waits for them, and re-layouts, place_block(): lax.dynamic_update_slice(buffer, fresh, (start, zero_column))  29.9 us
  transfers between devices with their start and end apart: 2, of which 1 were waited for; matrix products, arithmetic and copies ran while one was open for 28% of the time, Pallas kernels for 0%

commit v1 on v0

v1 whole, which is shorter than its diff:
```python
import functools

import jax
import jax.numpy as jnp
from jax import lax
from jax.experimental import pallas as pl
from jax.experimental.pallas import tpu as pltpu
from jax.sharding import PartitionSpec as P

HEAD_DIM = 128
MAX_STRETCHES = 8
CHUNKS = 4
LOG2_E = 1.4426950408889634
LOW = -1e30


def lookup(table, position):
    entries = jnp.arange(table.shape[0], dtype=jnp.int32)
    return jnp.sum(jnp.where(position[..., None] == entries, table, 0), axis=-1)


def attend_kernel(chunk, heads, info, q_ref, kv_hbm, w_hbm, out_ref, kv, w, q2, top, acc, att, kv_sem, w_sem):
    groups, rows = q_ref.shape[0], q_ref.shape[2]
    count = groups * rows
    stretch = kv.shape[1]
    mine, length = info[0], info[1]
    live = mine * stretch < length
    scale = HEAD_DIM ** (-0.5) * LOG2_E

    @pl.when(jnp.logical_not(live))
    def _():
        out_ref[...] = jnp.zeros_like(out_ref)

    @pl.when(live)
    def _():
        def fetch(i):
            return pltpu.make_async_copy(kv_hbm.at[info[2 + i]], kv.at[i, :, pl.ds(0, 2 * HEAD_DIM)], kv_sem.at[i])

        w_copy = pltpu.make_async_copy(w_hbm, w, w_sem)

        @pl.loop(0, mine + 1)
        def _(i):
            fetch(i).start()

        w_copy.start()
        for i in range(MAX_STRETCHES):
            kv[i, :, 2 * HEAD_DIM :] = jnp.ones((stretch, HEAD_DIM), jnp.bfloat16)
        for h in range(heads):
            q2[h * count : (h + 1) * count, :] = q_ref[:, 0, :, h * HEAD_DIM : (h + 1) * HEAD_DIM].reshape(
                count, HEAD_DIM
            )
        top[...] = jnp.full_like(top, LOW)
        acc[...] = jnp.zeros_like(acc)
        tile = 2 * count

        def block(i, diagonal):
            key = kv[i, :, 0:HEAD_DIM]
            value = kv[i, :, HEAD_DIM:]
            for t in range(heads * count // tile):
                part = slice(t * tile, (t + 1) * tile)
                scores = lax.dot_general(
                    q2[part, :], key, (((1,), (1,)), ((), ())), preferred_element_type=jnp.float32
                )
                if diagonal:
                    r = lax.broadcasted_iota(jnp.int32, (tile, stretch), 0) % count
                    at = r // rows * (CHUNKS * rows) + chunk * rows + r % rows
                    scores = jnp.where(lax.broadcasted_iota(jnp.int32, (tile, stretch), 1) <= at, scores, LOW)
                old = top[part, :]
                new = jnp.maximum(old, jnp.max(scores, axis=-1, keepdims=True) * scale)
                weights = jnp.exp2(scores * scale - jnp.concatenate([new] * (stretch // HEAD_DIM), axis=1))
                shrink = jnp.exp2(old - new)
                acc[part, :] = acc[part, :] * jnp.concatenate([shrink, shrink], axis=1) + jnp.dot(
                    weights.astype(jnp.bfloat16), value, preferred_element_type=jnp.float32
                )
                top[part, :] = new

        @pl.loop(0, mine)
        def _(i):
            fetch(i).wait()
            block(i, False)

        fetch(mine).wait()
        block(mine, True)

        r = lax.broadcasted_iota(jnp.int32, (count, HEAD_DIM), 0)
        at = mine * stretch + r // rows * (CHUNKS * rows) + chunk * rows + r % rows
        keep = (at < length).astype(jnp.float32)
        for h in range(heads):
            part = slice(h * count, (h + 1) * count)
            att[:, h * HEAD_DIM : (h + 1) * HEAD_DIM] = (
                acc[part, :HEAD_DIM] / acc[part, HEAD_DIM:] * keep
            ).astype(jnp.bfloat16)
        w_copy.wait()
        width = 1024
        for n in range(w.shape[1] // width):
            out_ref[:, n * width : (n + 1) * width] = jnp.dot(
                att[...], w[:, n * width : (n + 1) * width], preferred_element_type=jnp.float32
            ).astype(jnp.bfloat16)


def attend(chunk, info, queries, gathered, w_out):
    groups, _, rows, columns = queries.shape
    replicas, stretch, width = gathered.shape
    heads = columns // HEAD_DIM
    count = groups * rows
    features = w_out.shape[1]
    return pl.pallas_call(
        functools.partial(attend_kernel, chunk, heads),
        grid_spec=pltpu.PrefetchScalarGridSpec(
            num_scalar_prefetch=1,
            grid=(1,),
            in_specs=[
                pl.BlockSpec((groups, 1, rows, columns), lambda i, info: (0, chunk, 0, 0)),
                pl.BlockSpec(memory_space=pl.ANY),
                pl.BlockSpec(memory_space=pl.ANY),
            ],
            out_specs=pl.BlockSpec((count, features), lambda i, info: (0, 0)),
            scratch_shapes=[
                pltpu.VMEM((MAX_STRETCHES, stretch, width + HEAD_DIM), jnp.bfloat16),
                pltpu.VMEM(w_out.shape, jnp.bfloat16),
                pltpu.VMEM((heads * count, HEAD_DIM), jnp.bfloat16),
                pltpu.VMEM((heads * count, HEAD_DIM), jnp.float32),
                pltpu.VMEM((heads * count, 2 * HEAD_DIM), jnp.float32),
                pltpu.VMEM((count, columns), jnp.bfloat16),
                pltpu.SemaphoreType.DMA((MAX_STRETCHES,)),
                pltpu.SemaphoreType.DMA,
            ],
        ),
        out_shape=jax.ShapeDtypeStruct((count, features), jnp.bfloat16),
        compiler_params=pltpu.CompilerParams(vmem_limit_bytes=48 * 1024 * 1024),
        cost_estimate=pl.CostEstimate(
            flops=2 * count * columns * (features + 8 * stretch * 2), bytes_accessed=12 << 20, transcendentals=0
        ),
        name="attend_rows",
    )(info, queries, gathered, w_out)


def place_kernel(info, kv_ref, keys_ref, values_ref):
    stretch = kv_ref.shape[1]
    r = lax.broadcasted_iota(jnp.int32, (stretch, HEAD_DIM), 0)
    live = pl.program_id(0) * stretch + r < info[0]
    keys_ref[...] = jnp.where(live, kv_ref[0, :, :HEAD_DIM], 0)
    values_ref[...] = jnp.where(live, kv_ref[0, :, HEAD_DIM:], 0)


def place(info, gathered):
    replicas, stretch, width = gathered.shape
    cache = jax.ShapeDtypeStruct((MAX_STRETCHES * stretch, HEAD_DIM), jnp.bfloat16)
    return pl.pallas_call(
        place_kernel,
        grid_spec=pltpu.PrefetchScalarGridSpec(
            num_scalar_prefetch=1,
            grid=(MAX_STRETCHES,),
            in_specs=[pl.BlockSpec((1, stretch, width), lambda i, info: (info[1 + i], 0, 0))],
            out_specs=[pl.BlockSpec((stretch, HEAD_DIM), lambda i, info: (i, 0))] * 2,
        ),
        out_shape=[cache, cache],
        cost_estimate=pl.CostEstimate(flops=0, bytes_accessed=4 << 20, transcendentals=0),
        name="place_cache",
    )(info, gathered)


def shards(queries, keys, values, w_out, lengths, stretch_owner, home_replica):
    stretch = queries.shape[0]
    groups = lax.axis_size("tp")
    me = lax.axis_index("sp").astype(jnp.int32)
    slots = jnp.arange(stretch_owner.shape[0], dtype=jnp.int32)
    my_slot = jnp.sum(jnp.where(stretch_owner == me, slots, 0))
    prompt = my_slot // MAX_STRETCHES
    by_prompt = stretch_owner.reshape(-1, MAX_STRETCHES)
    prompts = jnp.arange(by_prompt.shape[0], dtype=jnp.int32)

    def owners(p):
        return jnp.sum(jnp.where((prompts == p)[:, None], by_prompt, 0), axis=0)

    info = jnp.concatenate([jnp.stack([my_slot % MAX_STRETCHES, lookup(lengths, prompt)]), owners(prompt)])
    homed = home_replica == me
    home_length = jnp.sum(jnp.where(homed, lengths, 0))
    home_prompt = jnp.sum(jnp.where(homed, prompts, 0))
    home_owners = jnp.where(jnp.any(homed), owners(home_prompt), 0)
    home_info = jnp.concatenate([home_length[None], home_owners])

    gathered = lax.all_gather(jnp.concatenate([keys, values], axis=1), "sp", axis=0)
    rows = stretch // groups // CHUNKS
    split = queries.reshape(groups, CHUNKS, rows, queries.shape[1])
    mixed = []
    for chunk in range(CHUNKS):
        partial = attend(chunk, info, split, gathered, w_out)
        mixed.append(lax.psum_scatter(partial, "tp", scatter_dimension=0, tiled=True))
    cache_keys, cache_values = place(home_info, gathered)
    return jnp.concatenate(mixed, axis=0), cache_keys, cache_values


def solution(mesh):
    placed = (P("sp", "tp"), P("sp", "tp"), P("sp", "tp"), P("tp", None), P(), P(), P())
    return jax.shard_map(
        shards,
        mesh=mesh,
        in_specs=placed,
        out_specs=(P(("sp", "tp"), None), P("sp", "tp"), P("sp", "tp")),
        check_vma=False,
    )
```

time: 546 us -> 251 us (0.46)
  loops' own time: 172 us -> 0 us
  other arithmetic: 157 us -> 10.1 us
  waiting for transfers between devices: 56.1 us -> 185 us
  local copies, waits for them, and re-layouts: 79.2 us -> 1.97 us
  matrix products: 61 us -> 0 us
  Pallas kernels: 0 us -> 33.1 us
    another operation x34 -> x0, loops' own time: 172 us -> none  [the longest x1 128 us: shards(): lax.scan(place_block, (empty_cache, empty_cache), (key_blocks, value_bloc...]
    reduce_scatter x1 -> x4, waiting for transfers between devices: 0.02 us -> 129 us  [shards(): lax.psum_scatter(partial, 'tp', scatter_dimension=0, tiled=True)]
    reduce_sum x139 -> x3, other arithmetic: 64.7 us -> 2.7 us  [the longest x1 1.32 us: shards(): home_length = jnp.sum(jnp.where(homed, lengths, 0))]
    dot_general x17 -> x0, matrix products: 61 us -> none  [the longest x8 32.3 us: update_block(): jnp.einsum('jfqm,mjy->jfqy', weights.astype(jnp.bfloat16), value_split, p...]
    dynamic_slice x64 -> x0, local copies, waits for them, and re-layouts: 37.5 us -> none  [shards(): lax.scan(step_block_update, start_state, (key_blocks, value_blocks, jnp.a...]
    select_n x96 -> x1, other arithmetic: 38.2 us -> 0.65 us  [shards(): home_owners = jnp.where(jnp.any(homed), owners(home_prompt), 0)]
    pallas_call x0 -> x5, Pallas kernels: none -> 33.1 us  [the longest x4 28.3 us: attend(): pl.pallas_call(functools.partial(attend_kernel, chunk, heads), grid_spec=...]
    dynamic_update_slice x64 -> x0, local copies, waits for them, and re-layouts: 29.9 us -> none  [place_block(): lax.dynamic_update_slice(buffer, fresh, (start, zero_column))]
  transfers between devices with their start and end apart: 2 -> 5, of which waited for: 1 -> 5; matrix products, arithmetic and copies ran while one was open for 28% -> 3% of each run, Pallas kernels for 0% -> 11%
where the time goes in v1:
time: 251 us; the launch traced here: 247 us
  waiting for transfers between devices  185 us (74%)
  Pallas kernels  33.1 us (13%)
  between operations  16.5 us (7%)
  other arithmetic  10.1 us (4%)
    reduce_scatter x4, waiting for transfers between devices, shards(): lax.psum_scatter(partial, 'tp', scatter_dimension=0, tiled=True)  129 us
    all_gather x1, waiting for transfers between devices, shards(): lax.all_gather(jnp.concatenate([keys, values], axis=1), 'sp', axis=0)  56.1 us
    pallas_call x4, Pallas kernels, attend(): pl.pallas_call(functools.partial(attend_kernel, chunk, heads), grid_spec=...  28.3 us
  transfers between devices with their start and end apart: 5, of which 5 were waited for; matrix products, arithmetic and copies ran while one was open for 3% of the time, Pallas kernels for 11%

profile of v1, /device:TPU:3, one launch (start us, length us, event | category | flops | bytes accessed | tf_op | source)
XLA Modules:
  0.0 247.2 jit_solution(11892267061393338952)
XLA Ops:
  7.2 1.7 pad_maximum_fusion.1
  8.9 0.0 reduce-scatter.11.cloned.1.call-start
  9.0 1.3 fusion
  12.9 0.7 reshape.21
  13.6 1.3 select_reduce_fusion.3
  14.9 0.6 iota_compare_fusion
  15.6 0.1 select_reduce_fusion
  15.7 0.6 pad_add_fusion.info
  16.3 56.1 %all-gather.3.cloned.1.call-done = bf16[16384,256]{1,0:T(8,128)(2,1)} async-done(((bf16[512,256]{1,0:T(8,128)(2,1)}), bf16[16384,256]{1,0:T(8,128)(2,1)}) %all-gather.3.cloned.1.call-update) | async-done | bytes 8388624 | tf_op jit(solution)/shard_map/all_gather | solution.py:183
  72.4 1.2 copy-done
  73.7 7.1 %attend_rows.7 = bf16[128,4096]{1,0:T(8,128)(2,1)} custom-call(s32[10]{0:T(128)S(1)} %pad_add_fusion.info, bf16[8,4,16,1024]{3,2,1,0:T(8,128)(2,1)S(1)} %bitcast.5, bf16[32,512,256]{2,1,0:T(8,128)(2,1)} %bitcast.9, bf16[1024,4096]{1,0:T(8,128)(2,1)} %w_hbm.7), custom_call_target="tpu_custom_call" | custom-call | flops 3221225472 | bytes 12582912 | tf_op jit(solution)/shard_map/attend_rows/pallas_call | solution.py:107
  80.8 0.0 reduce-scatter.5.cloned.1.call-start
  80.8 7.0 %attend_rows.4 = bf16[128,4096]{1,0:T(8,128)(2,1)} custom-call(s32[10]{0:T(128)S(1)} %pad_add_fusion.info, bf16[8,4,16,1024]{3,2,1,0:T(8,128)(2,1)S(1)} %bitcast.6, bf16[32,512,256]{2,1,0:T(8,128)(2,1)} %bitcast.10, bf16[1024,4096]{1,0:T(8,128)(2,1)} %w_hbm.7), custom_call_target="tpu_custom_call" | custom-call | flops 3221225472 | bytes 12582912 | tf_op jit(solution)/shard_map/attend_rows/pallas_call | solution.py:107
  87.9 7.0 %attend_rows.5 = bf16[128,4096]{1,0:T(8,128)(2,1)} custom-call(s32[10]{0:T(128)S(1)} %pad_add_fusion.info, bf16[8,4,16,1024]{3,2,1,0:T(8,128)(2,1)S(1)} %bitcast.7, bf16[32,512,256]{2,1,0:T(8,128)(2,1)} %bitcast.11, bf16[1024,4096]{1,0:T(8,128)(2,1)} %w_hbm.7), custom_call_target="tpu_custom_call" | custom-call | flops 3221225472 | bytes 12582912 | tf_op jit(solution)/shard_map/attend_rows/pallas_call | solution.py:107
  95.0 7.2 %attend_rows.6 = bf16[128,4096]{1,0:T(8,128)(2,1)} custom-call(s32[10]{0:T(128)S(1)} %pad_add_fusion.info, bf16[8,4,16,1024]{3,2,1,0:T(8,128)(2,1)S(1)} %bitcast.8, bf16[32,512,256]{2,1,0:T(8,128)(2,1)} %bitcast.12, bf16[1024,4096]{1,0:T(8,128)(2,1)} %w_hbm.7), custom_call_target="tpu_custom_call" | custom-call | flops 3221225472 | bytes 12582912 | tf_op jit(solution)/shard_map/attend_rows/pallas_call | solution.py:107
  102.3 0.6 fusion.2
  102.9 0.6 broadcast_select_fusion
  103.5 1.2 pad_add_fusion.1.info
  104.8 4.8 %place_cache.1 = (bf16[4096,128]{1,0:T(8,128)(2,1)}, bf16[4096,128]{1,0:T(8,128)(2,1)}) custom-call(s32[9]{0:T(128)} %pad_add_fusion.1.info, bf16[32,512,256]{2,1,0:T(8,128)(2,1)} %bitcast.13), custom_call_target="tpu_custom_call" | custom-call | bytes 4194304 | tf_op jit(solution)/shard_map/place_cache/pallas_call | solution.py:149
  109.6 9.5 %reduce-scatter.11.cloned.1.call-done = bf16[16,4096]{1,0:T(8,128)(2,1)} async-done(((bf16[128,4096]{1,0:T(8,128)(2,1)}), bf16[16,4096]{1,0:T(8,128)(2,1)}) %reduce-scatter.11.cloned.1.call-update) | async-done | bytes 131088 | tf_op jit(solution)/shard_map/reduce_scatter | solution.py:189
  119.1 40.0 %reduce-scatter.5.cloned.1.call-done = bf16[16,4096]{1,0:T(8,128)(2,1)} async-done(((bf16[128,4096]{1,0:T(8,128)(2,1)}), bf16[16,4096]{1,0:T(8,128)(2,1)}) %reduce-scatter.5.cloned.1.call-update) | async-done | bytes 131088 | tf_op jit(solution)/shard_map/reduce_scatter | solution.py:189
  159.1 39.9 %reduce-scatter.7.cloned.1.call-done = bf16[16,4096]{1,0:T(8,128)(2,1)} async-done(((bf16[128,4096]{1,0:T(8,128)(2,1)}), bf16[16,4096]{1,0:T(8,128)(2,1)}) %reduce-scatter.7.cloned.1.call-update) | async-done | bytes 131088 | tf_op jit(solution)/shard_map/reduce_scatter | solution.py:189
  199.0 39.8 %reduce-scatter.9.cloned.1.call-done = bf16[16,4096]{1,0:T(8,128)(2,1)} async-done(((bf16[128,4096]{1,0:T(8,128)(2,1)}), bf16[16,4096]{1,0:T(8,128)(2,1)}) %reduce-scatter.9.cloned.1.call-update) | async-done | bytes 131088 | tf_op jit(solution)/shard_map/reduce_scatter | solution.py:189
  238.8 1.9 pad_maximum_fusion
  (13 shorter events, 0.2 us)
Async XLA Ops:
  7.2 65.3 %all-gather.3.cloned.1.call-start = ((), (), s32[]{:S(2)}) async-start(), calls=%async_computation.8 | async-start | bytes 8650752 | tf_op jit(solution)/shard_map/all_gather | solution.py:183
  8.9 110.2 %reduce-scatter.11.cloned.1.call-start = ((), (), s32[]{:S(2)}) async-start(), calls=%async_computation.7 | async-start | bytes 1179648 | tf_op jit(solution)/shard_map/reduce_scatter | solution.py:189
  72.4 1.2 copy-start
  73.7 7.2 %copy-start.1 = (bf16[512,1024]{1,0:T(8,128)(2,1)S(1)}, bf16[512,1024]{1,0:T(8,128)(2,1)}, u32[]{:S(2)}) copy-start(bf16[512,1024]{1,0:T(8,128)(2,1)} %param.7) | copy-start | bytes 3145732
  80.8 78.4 %reduce-scatter.5.cloned.1.call-start = ((), (), s32[]{:S(2)}) async-start(), calls=%async_computation.4 | async-start | bytes 1179648 | tf_op jit(solution)/shard_map/reduce_scatter | solution.py:189
  87.9 111.1 %reduce-scatter.7.cloned.1.call-start = ((), (), s32[]{:S(2)}) async-start(), calls=%async_computation.5 | async-start | bytes 1179648 | tf_op jit(solution)/shard_map/reduce_scatter | solution.py:189
  94.9 7.3 %copy-start.2 = (s32[4]{0:T(128)S(1)}, s32[4]{0:T(128)}, u32[]{:S(2)}) copy-start(s32[4]{0:T(128)} %param.13) | copy-start | bytes 52
  95.0 143.8 %reduce-scatter.9.cloned.1.call-start = ((), (), s32[]{:S(2)}) async-start(), calls=%async_computation.6 | async-start | bytes 1179648 | tf_op jit(solution)/shard_map/reduce_scatter | solution.py:189
Sparse Core Ops, SparseCore 0:
  11.1 61.2 all-gather.2
  80.9 38.1 reduce-scatter.10
  121.7 37.4 reduce-scatter.4
  161.5 37.4 reduce-scatter.6
  201.4 37.3 reduce-scatter.8

commit v2 on v1

--- a/solution.py
+++ b/solution.py
@@ -9,7 +9,6 @@
 
 HEAD_DIM = 128
 MAX_STRETCHES = 8
-CHUNKS = 4
 LOG2_E = 1.4426950408889634
 LOW = -1e30
 
@@ -19,9 +18,8 @@
     return jnp.sum(jnp.where(position[..., None] == entries, table, 0), axis=-1)
 
 
-def attend_kernel(chunk, heads, info, q_ref, kv_hbm, w_hbm, out_ref, kv, w, q2, top, acc, att, kv_sem, w_sem):
-    groups, rows = q_ref.shape[0], q_ref.shape[2]
-    count = groups * rows
+def attend_kernel(heads, info, q_ref, kv_hbm, w_hbm, out_ref, kv, w, q2, top, acc, att, kv_sem, w_sem):
+    count = q_ref.shape[0]
     stretch = kv.shape[1]
     mine, length = info[0], info[1]
     live = mine * stretch < length
@@ -46,31 +44,31 @@
         for i in range(MAX_STRETCHES):
             kv[i, :, 2 * HEAD_DIM :] = jnp.ones((stretch, HEAD_DIM), jnp.bfloat16)
         for h in range(heads):
-            q2[h * count : (h + 1) * count, :] = q_ref[:, 0, :, h * HEAD_DIM : (h + 1) * HEAD_DIM].reshape(
-                count, HEAD_DIM
-            )
+            q2[h * count : (h + 1) * count, :] = q_ref[:, h * HEAD_DIM : (h + 1) * HEAD_DIM]
         top[...] = jnp.full_like(top, LOW)
         acc[...] = jnp.zeros_like(acc)
-        tile = 2 * count
+        tile = min(256, count)
 
         def block(i, diagonal):
-            key = kv[i, :, 0:HEAD_DIM]
-            value = kv[i, :, HEAD_DIM:]
             for t in range(heads * count // tile):
                 part = slice(t * tile, (t + 1) * tile)
+                first = t * tile % count
+                seen = first + tile if diagonal else stretch
                 scores = lax.dot_general(
-                    q2[part, :], key, (((1,), (1,)), ((), ())), preferred_element_type=jnp.float32
+                    q2[part, :],
+                    kv[i, :seen, :HEAD_DIM],
+                    (((1,), (1,)), ((), ())),
+                    preferred_element_type=jnp.float32,
                 )
                 if diagonal:
-                    r = lax.broadcasted_iota(jnp.int32, (tile, stretch), 0) % count
-                    at = r // rows * (CHUNKS * rows) + chunk * rows + r % rows
-                    scores = jnp.where(lax.broadcasted_iota(jnp.int32, (tile, stretch), 1) <= at, scores, LOW)
+                    at = lax.broadcasted_iota(jnp.int32, (tile, seen), 0) + first
+                    scores = jnp.where(lax.broadcasted_iota(jnp.int32, (tile, seen), 1) <= at, scores, LOW)
                 old = top[part, :]
                 new = jnp.maximum(old, jnp.max(scores, axis=-1, keepdims=True) * scale)
-                weights = jnp.exp2(scores * scale - jnp.concatenate([new] * (stretch // HEAD_DIM), axis=1))
+                weights = jnp.exp2(scores * scale - jnp.concatenate([new] * (seen // HEAD_DIM), axis=1))
                 shrink = jnp.exp2(old - new)
                 acc[part, :] = acc[part, :] * jnp.concatenate([shrink, shrink], axis=1) + jnp.dot(
-                    weights.astype(jnp.bfloat16), value, preferred_element_type=jnp.float32
+                    weights.astype(jnp.bfloat16), kv[i, :seen, HEAD_DIM:], preferred_element_type=jnp.float32
                 )
                 top[part, :] = new
 
@@ -83,7 +81,7 @@
         block(mine, True)
 
         r = lax.broadcasted_iota(jnp.int32, (count, HEAD_DIM), 0)
-        at = mine * stretch + r // rows * (CHUNKS * rows) + chunk * rows + r % rows
+        at = mine * stretch + r
         keep = (at < length).astype(jnp.float32)
         for h in range(heads):
             part = slice(h * count, (h + 1) * count)
@@ -98,19 +96,18 @@
             ).astype(jnp.bfloat16)
 
 
-def attend(chunk, info, queries, gathered, w_out):
-    groups, _, rows, columns = queries.shape
+def attend(info, queries, gathered, w_out):
+    count, columns = queries.shape
     replicas, stretch, width = gathered.shape
     heads = columns // HEAD_DIM
-    count = groups * rows
     features = w_out.shape[1]
     return pl.pallas_call(
-        functools.partial(attend_kernel, chunk, heads),
+        functools.partial(attend_kernel, heads),
         grid_spec=pltpu.PrefetchScalarGridSpec(
             num_scalar_prefetch=1,
             grid=(1,),
             in_specs=[
-                pl.BlockSpec((groups, 1, rows, columns), lambda i, info: (0, chunk, 0, 0)),
+                pl.BlockSpec((count, columns), lambda i, info: (0, 0)),
                 pl.BlockSpec(memory_space=pl.ANY),
                 pl.BlockSpec(memory_space=pl.ANY),
             ],
@@ -161,8 +158,6 @@
 
 
 def shards(queries, keys, values, w_out, lengths, stretch_owner, home_replica):
-    stretch = queries.shape[0]
-    groups = lax.axis_size("tp")
     me = lax.axis_index("sp").astype(jnp.int32)
     slots = jnp.arange(stretch_owner.shape[0], dtype=jnp.int32)
     my_slot = jnp.sum(jnp.where(stretch_owner == me, slots, 0))
@@ -181,14 +176,10 @@
     home_info = jnp.concatenate([home_length[None], home_owners])
 
     gathered = lax.all_gather(jnp.concatenate([keys, values], axis=1), "sp", axis=0)
-    rows = stretch // groups // CHUNKS
-    split = queries.reshape(groups, CHUNKS, rows, queries.shape[1])
-    mixed = []
-    for chunk in range(CHUNKS):
-        partial = attend(chunk, info, split, gathered, w_out)
-        mixed.append(lax.psum_scatter(partial, "tp", scatter_dimension=0, tiled=True))
+    partial = attend(info, queries, gathered, w_out)
+    mixed = lax.psum_scatter(partial, "tp", scatter_dimension=0, tiled=True)
     cache_keys, cache_values = place(home_info, gathered)
-    return jnp.concatenate(mixed, axis=0), cache_keys, cache_values
+    return mixed, cache_keys, cache_values
 
 
 def solution(mesh):

time: 251 us -> 166 us (0.66)
  waiting for transfers between devices: 185 us -> 105 us
  Pallas kernels: 33.1 us -> 30.3 us
    reduce_scatter x4 -> x1, waiting for transfers between devices: 129 us -> 48.7 us  [shards(): mixed = lax.psum_scatter(partial, 'tp', scatter_dimension=0, tiled=True)]
    pallas_call x4 -> x1, Pallas kernels: 28.3 us -> 23.8 us  [attend(): pl.pallas_call(functools.partial(attend_kernel, heads), grid_spec=pltpu.P...]
  transfers between devices with their start and end apart: 5 -> 2, of which waited for: 5 -> 2; matrix products, arithmetic and copies ran while one was open for 3% -> 4% of each run, Pallas kernels for 11% -> 4%
where the time goes in v2:
time: 166 us; the launch traced here: 164 us
  waiting for transfers between devices  105 us (63%)
  Pallas kernels  30.3 us (18%)
  between operations  16.7 us (10%)
  other arithmetic  8.24 us (5%)
  local copies, waits for them, and re-layouts  3.93 us (2%)
    all_gather x1, waiting for transfers between devices, shards(): lax.all_gather(jnp.concatenate([keys, values], axis=1), 'sp', axis=0)  56.1 us
    reduce_scatter x1, waiting for transfers between devices, shards(): mixed = lax.psum_scatter(partial, 'tp', scatter_dimension=0, tiled=True)  48.7 us
    pallas_call x1, Pallas kernels, attend(): pl.pallas_call(functools.partial(attend_kernel, heads), grid_spec=pltpu.P...  23.8 us
    pallas_call x1, Pallas kernels, place(): pl.pallas_call(place_kernel, grid_spec=pltpu.PrefetchScalarGridSpec(num_s...  6.54 us
  transfers between devices with their start and end apart: 2, of which 2 were waited for; matrix products, arithmetic and copies ran while one was open for 4% of the time, Pallas kernels for 4%

profile of v2, /device:TPU:3, one launch (start us, length us, event | category | flops | bytes accessed | tf_op | source)
XLA Modules:
  0.0 164.1 jit_solution(13895938866223322938)
XLA Ops:
  7.2 0.0 all-gather.3.cloned.1.call-start
  7.2 1.7 %pad_maximum_fusion = bf16[512,256]{1,0:T(8,128)(2,1)} fusion(bf16[512,128]{1,0:T(8,128)(2,1)} %param.9, bf16[512,128]{1,0:T(8,128)(2,1)} %param.8), kind=kLoop, calls=%fused_computation | loop fusion | flops 524288 | bytes 524288 | tf_op jit(solution)/shard_map/concatenate | solution.py:178
  8.9 0.0 all-gather.3.cloned.1.call-update
  8.9 0.0 reduce-scatter.2.cloned.1.call-start
  9.0 1.3 fusion
  12.9 0.7 reshape.18
  13.6 1.3 select_reduce_fusion.3
  14.9 0.6 iota_compare_fusion
  15.6 0.1 select_reduce_fusion
  15.7 0.6 pad_add_fusion.info
  16.3 56.1 %all-gather.3.cloned.1.call-done = bf16[16384,256]{1,0:T(8,128)(2,1)} async-done(((bf16[512,256]{1,0:T(8,128)(2,1)}), bf16[16384,256]{1,0:T(8,128)(2,1)}) %all-gather.3.cloned.1.call-update) | async-done | bytes 8388624 | tf_op jit(solution)/shard_map/all_gather | solution.py:178
  72.4 0.0 copy-start.1
  72.4 1.2 copy-done.1
  73.7 0.0 copy-start.2
  73.7 23.8 %attend_rows.1 = bf16[512,4096]{1,0:T(8,128)(2,1)S(1)} custom-call(s32[10]{0:T(128)S(1)} %pad_add_fusion.info, bf16[512,1024]{1,0:T(8,128)(2,1)S(1)} %copy-done.1, bf16[32,512,256]{2,1,0:T(8,128)(2,1)} %bitcast.4, bf16[1024,4096]{1,0:T(8,128)(2,1)} %w_hbm.1), custom_call_target="tpu_custom_call" | custom-call | flops 12884901888 | bytes 12582912 | tf_op jit(solution)/shard_map/attend_rows/pallas_call | solution.py:104
  97.4 0.0 copy-start
  97.5 2.0 %copy-done = bf16[512,4096]{1,0:T(8,128)(2,1)} copy-done((bf16[512,4096]{1,0:T(8,128)(2,1)}, bf16[512,4096]{1,0:T(8,128)(2,1)S(1)}, u32[]{:S(2)}) %copy-start) | copy-done | bytes 4194328
  99.4 0.0 reduce-scatter.2.cloned.1.call-update
  99.4 0.0 copy-done.2
  99.5 0.6 fusion.2
  100.1 0.6 broadcast_select_fusion
  100.7 1.3 pad_add_fusion.1.info
  102.0 6.5 %place_cache.1 = (bf16[4096,128]{1,0:T(8,128)(2,1)}, bf16[4096,128]{1,0:T(8,128)(2,1)}) custom-call(s32[9]{0:T(128)} %pad_add_fusion.1.info, bf16[32,512,256]{2,1,0:T(8,128)(2,1)} %bitcast.5), custom_call_target="tpu_custom_call" | custom-call | bytes 4194304 | tf_op jit(solution)/shard_map/place_cache/pallas_call | solution.py:146
  108.5 48.7 %reduce-scatter.2.cloned.1.call-done = bf16[64,4096]{1,0:T(8,128)(2,1)} async-done(((bf16[512,4096]{1,0:T(8,128)(2,1)}), bf16[64,4096]{1,0:T(8,128)(2,1)}) %reduce-scatter.2.cloned.1.call-update) | async-done | bytes 524304 | tf_op jit(solution)/shard_map/reduce_scatter | solution.py:180
Async XLA Ops:
  7.2 65.3 %all-gather.3.cloned.1.call-start = ((), (), s32[]{:S(2)}) async-start(), calls=%async_computation.2 | async-start | bytes 8650752 | tf_op jit(solution)/shard_map/all_gather | solution.py:178
  8.9 148.4 %reduce-scatter.2.cloned.1.call-start = ((), (), s32[]{:S(2)}) async-start(), calls=%async_computation.1 | async-start | bytes 4718592 | tf_op jit(solution)/shard_map/reduce_scatter | solution.py:180
  72.4 1.2 copy-start.1
  73.7 25.8 %copy-start.2 = (s32[4]{0:T(128)S(1)}, s32[4]{0:T(128)}, u32[]{:S(2)}) copy-start(s32[4]{0:T(128)} %param.13) | copy-start | bytes 52
  97.4 2.0 %copy-start = (bf16[512,4096]{1,0:T(8,128)(2,1)}, bf16[512,4096]{1,0:T(8,128)(2,1)S(1)}, u32[]{:S(2)}) copy-start(bf16[512,4096]{1,0:T(8,128)(2,1)S(1)} %attend_rows.1) | copy-start | bytes 12582916
Sparse Core Ops, SparseCore 0:
  11.1 61.2 all-gather.2
  99.6 57.6 reduce-scatter.1

commit v3 on v2

v3 whole, which is shorter than its diff:
```python
import functools

import jax
import jax.numpy as jnp
from jax import lax
from jax.experimental import pallas as pl
from jax.experimental.pallas import tpu as pltpu
from jax.sharding import PartitionSpec as P

HEAD_DIM = 128
MAX_STRETCHES = 8
SIDE = 4
LOG2_E = 1.4426950408889634
LOW = -1e30


def find(table, wanted, missing):
    return lax.fori_loop(
        0, table.shape[0], lambda j, found: jnp.where(table[j] == wanted, j, found), jnp.int32(missing)
    )


def held_at(me, owner):
    dx = lax.rem(owner // (2 * SIDE) - me // (2 * SIDE) + SIDE, SIDE)
    dy = lax.rem(lax.rem(owner // 2, SIDE) - lax.rem(me // 2, SIDE) + SIDE, SIDE)
    other = lax.rem(owner + me, 2)
    first = lax.rem(me, 2) == 0
    return jnp.where(first, dy, dx), jnp.where(first, dx, dy) * 2 + other


def start_half(pieces, piece, slot, target, sem):
    for p, ref in enumerate(pieces):

        @pl.when(piece == p)
        def _():
            pltpu.make_async_copy(ref.at[slot], target, sem).start()


def pick_kernel(home, me_ref, lengths, stretch_owner, home_replica, *refs):
    pieces, out, sem = refs[:SIDE], refs[SIDE], refs[SIDE + 1]
    me = me_ref[0]
    other = me + 1 - 2 * lax.rem(me, 2)
    if home:
        prompt = find(home_replica, other, 0)
    else:
        prompt = find(stretch_owner, other, 0) // MAX_STRETCHES
    for i in range(MAX_STRETCHES):
        piece, slot = held_at(me, stretch_owner[prompt * MAX_STRETCHES + i])
        start_half(pieces, piece, slot, out.at[i], sem.at[i])
    for i in range(MAX_STRETCHES):
        pltpu.make_async_copy(pieces[0].at[0], out.at[i], sem.at[i]).wait()


def pick(home, scalars, pieces):
    shape = (MAX_STRETCHES,) + pieces[0].shape[1:]
    return pl.pallas_call(
        functools.partial(pick_kernel, home),
        grid_spec=pltpu.PrefetchScalarGridSpec(
            num_scalar_prefetch=len(scalars),
            grid=(1,),
            in_specs=[pl.BlockSpec(memory_space=pl.ANY)] * SIDE,
            out_specs=pl.BlockSpec(memory_space=pl.ANY),
            scratch_shapes=[pltpu.SemaphoreType.DMA((MAX_STRETCHES,))],
        ),
        out_shape=jax.ShapeDtypeStruct(shape, jnp.bfloat16),
        compiler_params=pltpu.CompilerParams(vmem_limit_bytes=1024 * 1024),
        cost_estimate=pl.CostEstimate(flops=0, bytes_accessed=2 << 20, transcendentals=0),
        name="pick_home" if home else "pick_visible",
    )(*scalars, *pieces)


def attend_kernel(heads, me_ref, lengths, stretch_owner, home_replica, q_ref, *refs):
    pieces = refs[:SIDE]
    other_hbm, w_hbm, out_ref, kv, w, q2, top, acc, att, own_sem, other_sem, w_sem = refs[SIDE:]
    count = q_ref.shape[0]
    stretch = kv.shape[1]
    half = stretch // 2
    me = me_ref[0]
    slot = find(stretch_owner, me, 0)
    prompt = slot // MAX_STRETCHES
    mine = lax.rem(slot, MAX_STRETCHES)
    length = lengths[prompt]
    live = mine * stretch < length
    scale = HEAD_DIM ** (-0.5) * LOG2_E
    own_rows = pl.ds(pl.multiple_of(lax.rem(me, 2) * half, half), half)
    other_rows = pl.ds(pl.multiple_of((1 - lax.rem(me, 2)) * half, half), half)
    columns = pl.ds(0, 2 * HEAD_DIM)

    @pl.when(jnp.logical_not(live))
    def _():
        out_ref[...] = jnp.zeros_like(out_ref)

    @pl.when(live)
    def _():
        def other_copy(i):
            return pltpu.make_async_copy(other_hbm.at[i], kv.at[i, other_rows, columns], other_sem.at[i])

        def arrive(i):
            pltpu.make_async_copy(pieces[0].at[0], kv.at[i, own_rows, columns], own_sem.at[i]).wait()
            other_copy(i).wait()

        @pl.loop(0, mine + 1)
        def _(i):
            piece, at = held_at(me, stretch_owner[prompt * MAX_STRETCHES + i])
            start_half(pieces, piece, at, kv.at[i, own_rows, columns], own_sem.at[i])
            other_copy(i).start()

        w_copy = pltpu.make_async_copy(w_hbm, w, w_sem)
        w_copy.start()
        for i in range(MAX_STRETCHES):
            kv[i, :, 2 * HEAD_DIM :] = jnp.ones((stretch, HEAD_DIM), jnp.bfloat16)
        for h in range(heads):
            q2[h * count : (h + 1) * count, :] = q_ref[:, h * HEAD_DIM : (h + 1) * HEAD_DIM]
        top[...] = jnp.full_like(top, LOW)
        acc[...] = jnp.zeros_like(acc)
        tile = min(256, count)

        def block(i, diagonal):
            for t in range(heads * count // tile):
                part = slice(t * tile, (t + 1) * tile)
                first = t * tile % count
                seen = first + tile if diagonal else stretch
                scores = lax.dot_general(
                    q2[part, :],
                    kv[i, :seen, :HEAD_DIM],
                    (((1,), (1,)), ((), ())),
                    preferred_element_type=jnp.float32,
                )
                if diagonal:
                    at = lax.broadcasted_iota(jnp.int32, (tile, seen), 0) + first
                    scores = jnp.where(lax.broadcasted_iota(jnp.int32, (tile, seen), 1) <= at, scores, LOW)
                old = top[part, :]
                new = jnp.maximum(old, jnp.max(scores, axis=-1, keepdims=True) * scale)
                weights = jnp.exp2(scores * scale - jnp.concatenate([new] * (seen // HEAD_DIM), axis=1))
                shrink = jnp.exp2(old - new)
                acc[part, :] = acc[part, :] * jnp.concatenate([shrink, shrink], axis=1) + jnp.dot(
                    weights.astype(jnp.bfloat16), kv[i, :seen, HEAD_DIM:], preferred_element_type=jnp.float32
                )
                top[part, :] = new

        @pl.loop(0, mine)
        def _(i):
            arrive(i)
            block(i, False)

        arrive(mine)
        block(mine, True)

        at = mine * stretch + lax.broadcasted_iota(jnp.int32, (count, HEAD_DIM), 0)
        keep = (at < length).astype(jnp.float32)
        for h in range(heads):
            part = slice(h * count, (h + 1) * count)
            att[:, h * HEAD_DIM : (h + 1) * HEAD_DIM] = (
                acc[part, :HEAD_DIM] / acc[part, HEAD_DIM:] * keep
            ).astype(jnp.bfloat16)
        w_copy.wait()
        width = 1024
        for n in range(w.shape[1] // width):
            out_ref[:, n * width : (n + 1) * width] = jnp.dot(
                att[...], w[:, n * width : (n + 1) * width], preferred_element_type=jnp.float32
            ).astype(jnp.bfloat16)


def attend(scalars, queries, pieces, other, w_out):
    count, columns = queries.shape
    _, half, width = other.shape
    heads = columns // HEAD_DIM
    features = w_out.shape[1]
    return pl.pallas_call(
        functools.partial(attend_kernel, heads),
        grid_spec=pltpu.PrefetchScalarGridSpec(
            num_scalar_prefetch=len(scalars),
            grid=(1,),
            in_specs=[pl.BlockSpec((count, columns), lambda i, *_: (0, 0))]
            + [pl.BlockSpec(memory_space=pl.ANY)] * (SIDE + 2),
            out_specs=pl.BlockSpec((count, features), lambda i, *_: (0, 0)),
            scratch_shapes=[
                pltpu.VMEM((MAX_STRETCHES, 2 * half, width + HEAD_DIM), jnp.bfloat16),
                pltpu.VMEM(w_out.shape, jnp.bfloat16),
                pltpu.VMEM((heads * count, HEAD_DIM), jnp.bfloat16),
                pltpu.VMEM((heads * count, HEAD_DIM), jnp.float32),
                pltpu.VMEM((heads * count, 2 * HEAD_DIM), jnp.float32),
                pltpu.VMEM((count, columns), jnp.bfloat16),
                pltpu.SemaphoreType.DMA((MAX_STRETCHES,)),
                pltpu.SemaphoreType.DMA((MAX_STRETCHES,)),
                pltpu.SemaphoreType.DMA,
            ],
        ),
        out_shape=jax.ShapeDtypeStruct((count, features), jnp.bfloat16),
        compiler_params=pltpu.CompilerParams(vmem_limit_bytes=48 * 1024 * 1024),
        cost_estimate=pl.CostEstimate(
            flops=2 * count * columns * (features + 4 * MAX_STRETCHES * half), bytes_accessed=16 << 20, transcendentals=0
        ),
        name="attend_rows",
    )(*scalars, queries, *pieces, other, w_out)


def place_kernel(me_ref, lengths, stretch_owner, home_replica, *refs):
    pieces = refs[:SIDE]
    other_hbm, keys_ref, values_ref, kv, own_sem, other_sem = refs[SIDE:]
    stretch = kv.shape[1]
    half = stretch // 2
    me = me_ref[0]
    prompt = find(home_replica, me, -1)
    homed = prompt >= 0

    @pl.when(jnp.logical_not(homed))
    def _():
        keys_ref[...] = jnp.zeros_like(keys_ref)
        values_ref[...] = jnp.zeros_like(values_ref)

    @pl.when(homed)
    def _():
        own_rows = pl.ds(pl.multiple_of(lax.rem(me, 2) * half, half), half)
        other_rows = pl.ds(pl.multiple_of((1 - lax.rem(me, 2)) * half, half), half)
        length = lengths[prompt]
        for i in range(MAX_STRETCHES):
            piece, slot = held_at(me, stretch_owner[prompt * MAX_STRETCHES + i])
            start_half(pieces, piece, slot, kv.at[i, own_rows], own_sem.at[i])
            pltpu.make_async_copy(other_hbm.at[i], kv.at[i, other_rows], other_sem.at[i]).start()
        for i in range(MAX_STRETCHES):
            pltpu.make_async_copy(pieces[0].at[0], kv.at[i, own_rows], own_sem.at[i]).wait()
            pltpu.make_async_copy(other_hbm.at[i], kv.at[i, other_rows], other_sem.at[i]).wait()
            live = i * stretch + lax.broadcasted_iota(jnp.int32, (stretch, HEAD_DIM), 0) < length
            rows = slice(i * stretch, (i + 1) * stretch)
            keys_ref[rows, :] = jnp.where(live, kv[i, :, :HEAD_DIM], 0)
            values_ref[rows, :] = jnp.where(live, kv[i, :, HEAD_DIM:], 0)


def place(scalars, pieces, other):
    _, half, width = other.shape
    rows = MAX_STRETCHES * 2 * half
    cache = jax.ShapeDtypeStruct((rows, HEAD_DIM), jnp.bfloat16)
    return pl.pallas_call(
        place_kernel,
        grid_spec=pltpu.PrefetchScalarGridSpec(
            num_scalar_prefetch=len(scalars),
            grid=(1,),
            in_specs=[pl.BlockSpec(memory_space=pl.ANY)] * (SIDE + 1),
            out_specs=[pl.BlockSpec((rows, HEAD_DIM), lambda i, *_: (0, 0))] * 2,
            scratch_shapes=[
                pltpu.VMEM((MAX_STRETCHES, 2 * half, width), jnp.bfloat16),
                pltpu.SemaphoreType.DMA((MAX_STRETCHES,)),
                pltpu.SemaphoreType.DMA((MAX_STRETCHES,)),
            ],
        ),
        out_shape=[cache, cache],
        compiler_params=pltpu.CompilerParams(vmem_limit_bytes=8 * 1024 * 1024),
        cost_estimate=pl.CostEstimate(flops=0, bytes_accessed=4 << 20, transcendentals=0),
        name="place_cache",
    )(*scalars, *pieces, other)


def route(first, step):
    pairs = []
    for x in range(SIDE):
        for y in range(SIDE):
            for core in range(2):
                along_x = (core == 0) == first
                sx, sy = ((x + step) % SIDE, y) if along_x else (x, (y + step) % SIDE)
                pairs.append(((sx * SIDE + sy) * 2 + core, (x * SIDE + y) * 2 + core))
    return pairs


def swap_cores(array):
    return lax.ppermute(array, "sp", [(r, r + 1 - 2 * (r % 2)) for r in range(2 * SIDE * SIDE)])


def gather_halves(keys, values):
    core = lax.axis_index("sp") % 2
    half = keys.shape[0] // 2
    both = jnp.concatenate([keys, values], axis=1)
    got = swap_cores(lax.dynamic_slice_in_dim(both, (1 - core) * half, half, 0))
    chip = jnp.stack([lax.dynamic_slice_in_dim(both, core * half, half, 0), got])
    line = jnp.concatenate([chip] + [lax.ppermute(chip, "sp", route(True, step)) for step in range(1, SIDE)], axis=0)
    return [line] + [lax.ppermute(line, "sp", route(False, step)) for step in range(1, SIDE)]


def shards(queries, keys, values, w_out, lengths, stretch_owner, home_replica):
    me = lax.axis_index("sp").astype(jnp.int32).reshape(1)
    scalars = (me, lengths, stretch_owner, home_replica)
    pieces = gather_halves(keys, values)
    other = swap_cores(pick(False, scalars, pieces))
    partial = attend(scalars, queries, pieces, other, w_out)
    mixed = lax.psum_scatter(partial, "tp", scatter_dimension=0, tiled=True)
    home_other = swap_cores(pick(True, scalars, pieces))
    cache_keys, cache_values = place(scalars, pieces, home_other)
    return mixed, cache_keys, cache_values


def solution(mesh):
    placed = (P("sp", "tp"), P("sp", "tp"), P("sp", "tp"), P("tp", None), P(), P(), P())
    return jax.shard_map(
        shards,
        mesh=mesh,
        in_specs=placed,
        out_specs=(P(("sp", "tp"), None), P("sp", "tp"), P("sp", "tp")),
        check_vma=False,
    )
```

time: 166 us -> 157 us (0.946)
  waiting for transfers between devices: 105 us -> 81.3 us
  starting transfers between devices: 0.08 us -> 11.7 us
  Pallas kernels: 30.3 us -> 39.9 us
  other arithmetic: 8.24 us -> 0.03 us
  local copies, waits for them, and re-layouts: 3.93 us -> 8.59 us
  between operations: 16.7 us -> 14.2 us
    all_gather x1 -> x0, waiting for transfers between devices: 56.1 us -> none  [shards(): lax.all_gather(jnp.concatenate([keys, values], axis=1), 'sp', axis=0)]
    ppermute x0 -> x9, waiting for transfers between devices: none -> 37.4 us  [the longest x3 23.1 us: gather_halves(): lax.ppermute(line, 'sp', route(False, step))]
    ppermute x0 -> x9, starting transfers between devices: none -> 11.7 us  [the longest x3 3.99 us: gather_halves(): lax.ppermute(line, 'sp', route(False, step))]
    pallas_call x1, Pallas kernels: 23.8 us -> 32.6 us  [attend(): pl.pallas_call(functools.partial(attend_kernel, heads), grid_spec=pltpu.P...]
    pallas_call x0 -> x2, Pallas kernels: none -> 4.97 us  [pick(): pl.pallas_call(functools.partial(pick_kernel, home), grid_spec=pltpu.Pref...]
    reduce_scatter x1, waiting for transfers between devices: 48.7 us -> 43.9 us  [shards(): mixed = lax.psum_scatter(partial, 'tp', scatter_dimension=0, tiled=True)]
    unnamed x6 -> x27, local copies, waits for them, and re-layouts: 3.2 us -> 7.62 us
    pallas_call x1, Pallas kernels: 6.54 us -> 2.32 us  [place(): pl.pallas_call(place_kernel, grid_spec=pltpu.PrefetchScalarGridSpec(num_s...]
  transfers between devices with their start and end apart: 2 -> 10, of which waited for: 2 -> 10; matrix products, arithmetic and copies ran while one was open for 4% -> 0% of each run, Pallas kernels for 4% -> 3%
where the time goes in v3:
time: 157 us; the launch traced here: 156 us
  waiting for transfers between devices  81.3 us (52%)
  Pallas kernels  39.9 us (25%)
  between operations  14.2 us (9%)
  starting transfers between devices  11.7 us (7%)
  local copies, waits for them, and re-layouts  8.59 us (5%)
    reduce_scatter x1, waiting for transfers between devices, shards(): mixed = lax.psum_scatter(partial, 'tp', scatter_dimension=0, tiled=True)  43.9 us
    pallas_call x1, Pallas kernels, attend(): pl.pallas_call(functools.partial(attend_kernel, heads), grid_spec=pltpu.P...  32.6 us
    ppermute x3, waiting for transfers between devices, gather_halves(): lax.ppermute(line, 'sp', route(False, step))  23.1 us
    ppermute x3, waiting for transfers between devices, gather_halves(): lax.ppermute(chip, 'sp', route(True, step))  8.44 us
    unnamed x27, local copies, waits for them, and re-layouts  7.62 us
    ppermute x3, waiting for transfers between devices, swap_cores(): lax.ppermute(array, 'sp', [(r, r + 1 - 2 * (r % 2)) for r in range(2 * SI...  5.9 us
    pallas_call x2, Pallas kernels, pick(): pl.pallas_call(functools.partial(pick_kernel, home), grid_spec=pltpu.Pref...  4.97 us
    ppermute x3, starting transfers between devices, gather_halves(): lax.ppermute(line, 'sp', route(False, step))  3.99 us
  transfers between devices with their start and end apart: 10, of which 10 were waited for; matrix products, arithmetic and copies ran while one was open for 0% of the time, Pallas kernels for 3%

profile of v3, /device:TPU:3, one launch (start us, length us, event | category | flops | bytes accessed | tf_op | source)
XLA Modules:
  0.0 155.7 jit_solution(11054245129926367848)
XLA Ops:
  7.2 0.9 constant_dynamic-update-slice_fusion.1
  8.2 0.9 constant_dynamic-update-slice_fusion
  9.2 0.8 collective-permute-start
  9.9 1.0 collective-permute-done
  10.9 2.8 %collective-permute-start.1 = (bf16[2,256,256]{2,1,0:T(8,128)(2,1)S(1)}, bf16[2,256,256]{2,1,0:T(8,128)(2,1)S(1)}, u32[]{:S(2)}, u32[]{:S(2)}) collective-permute-start(bf16[2,256,256]{2,1,0:T(8,128)(2,1)S(1)} %pad_maximum_fusion), channel_id=1, source_target_pairs={{64,0},{24,8},{80,16},{40,24},{96,32},{56,40},{112,48},{8,56},{128... | collective-permute-start | bytes 786440 | tf_op jit(solution)/shard_map/ppermute | solution.py:275
  14.8 5.1 %collective-permute-done.1 = bf16[2,256,256]{2,1,0:T(8,128)(2,1)S(1)} collective-permute-done((bf16[2,256,256]{2,1,0:T(8,128)(2,1)S(1)}, bf16[2,256,256]{2,1,0:T(8,128)(2,1)S(1)}, u32[]{:S(2)}, u32[]{:S(2)}) %collective-permute-start.1) | collective-permute-done | bytes 262176 | tf_op jit(solution)/shard_map/ppermute | solution.py:275
  20.6 2.7 %collective-permute-done.3 = bf16[2,256,256]{2,1,0:T(8,128)(2,1)S(1)} collective-permute-done((bf16[2,256,256]{2,1,0:T(8,128)(2,1)S(1)}, bf16[2,256,256]{2,1,0:T(8,128)(2,1)S(1)}, u32[]{:S(2)}, u32[]{:S(2)}) %collective-permute-start.3) | collective-permute-done | bytes 262176 | tf_op jit(solution)/shard_map/ppermute | solution.py:275
  23.9 1.8 %collective-permute-start.5 = (bf16[8,256,256]{2,1,0:T(8,128)(2,1)S(1)}, bf16[8,256,256]{2,1,0:T(8,128)(2,1)S(1)}, u32[]{:S(2)}, u32[]{:S(2)}) collective-permute-start(bf16[8,256,256]{2,1,0:T(8,128)(2,1)S(1)} %constant_dynamic-update-slice_fusion.2.refs_0_), channel_id=1, source_target_pairs={{32,0},{136,8},{48,16},{152,24},{0,32},{168,40},{16,48},{184,56},{... | collective-permute-start | bytes 3145736 | tf_op jit(solution)/shard_map/ppermute | solution.py:276
  25.8 1.5 collective-permute-start.6
  27.3 10.0 %collective-permute-done.4.refs_1_ = bf16[8,256,256]{2,1,0:T(8,128)(2,1)S(1)} collective-permute-done((bf16[8,256,256]{2,1,0:T(8,128)(2,1)S(1)}, bf16[8,256,256]{2,1,0:T(8,128)(2,1)S(1)}, u32[]{:S(2)}, u32[]{:S(2)}) %collective-permute-start.4) | collective-permute-done | bytes 1048608 | tf_op jit(solution)/shard_map/ppermute | solution.py:276
  37.3 12.2 %collective-permute-done.5.refs_2_ = bf16[8,256,256]{2,1,0:T(8,128)(2,1)S(1)} collective-permute-done((bf16[8,256,256]{2,1,0:T(8,128)(2,1)S(1)}, bf16[8,256,256]{2,1,0:T(8,128)(2,1)S(1)}, u32[]{:S(2)}, u32[]{:S(2)}) %collective-permute-start.5) | collective-permute-done | bytes 1048608 | tf_op jit(solution)/shard_map/ppermute | solution.py:276
  49.5 0.9 collective-permute-done.6.refs_3_
  52.4 2.6 %pick_visible.1 = bf16[8,256,256]{2,1,0:T(8,128)(2,1)S(1)} custom-call(s32[1]{0:T(128)} %bitcast.me_ref, s32[4]{0:T(128)S(1)} %copy-done.3, s32[32]{0:T(128)S(1)} %copy-done.5, s32[4]{0:T(128)S(1)} %copy-done.7, bf16[8,256,256]{2,1,0:T(8,128)(2,1)S(1)} %constant_dynamic-update-slice_fusion.2.refs_0_, ...), custom_call_target="tpu_custom_call" | custom-call | bytes 2097152 | tf_op jit(solution)/shard_map/pick_visible/pallas_call | solution.py:56
  55.0 3.0 %collective-permute-start.7 = (bf16[8,256,256]{2,1,0:T(8,128)(2,1)S(1)}, bf16[8,256,256]{2,1,0:T(8,128)(2,1)S(1)}, u32[]{:S(2)}, u32[]{:S(2)}) collective-permute-start(bf16[8,256,256]{2,1,0:T(8,128)(2,1)S(1)} %pick_visible.1), channel_id=1, source_target_pairs={{0,8},{8,0},{16,24},{24,16},{32,40},{40,32},{48,56},{56,48},{64,72... | collective-permute-start | bytes 3145736 | tf_op jit(solution)/shard_map/ppermute | solution.py:266
  58.0 2.3 %collective-permute-done.7.refs_4_ = bf16[8,256,256]{2,1,0:T(8,128)(2,1)S(1)} collective-permute-done((bf16[8,256,256]{2,1,0:T(8,128)(2,1)S(1)}, bf16[8,256,256]{2,1,0:T(8,128)(2,1)S(1)}, u32[]{:S(2)}, u32[]{:S(2)}) %collective-permute-start.7) | collective-permute-done | bytes 1048608 | tf_op jit(solution)/shard_map/ppermute | solution.py:266
  60.3 1.0 copy-done.10
  61.3 1.2 copy-done.9
  62.5 32.6 %attend_rows.1 = bf16[512,4096]{1,0:T(8,128)(2,1)} custom-call(s32[1]{0:T(128)} %bitcast.me_ref, s32[4]{0:T(128)S(1)} %copy-done.4, s32[32]{0:T(128)S(1)} %copy-done.6, s32[4]{0:T(128)S(1)} %copy-done.7, bf16[512,1024]{1,0:T(8,128)(2,1)S(1)} %copy-done.9, bf16[8,256,256]{2,1,0:T(8,128)(2,1)S(1)} %constant_dynamic-update-slice_fusion.2.refs_0_, ...), custom_call_target="tpu_custom_call" | custom-call | flops 12884901888 | bytes 16777216 | tf_op jit(solution)/shard_map/attend_rows/pallas_call | solution.py:169
  95.1 1.2 copy-done.1
  96.3 2.3 %pick_home.1 = bf16[8,256,256]{2,1,0:T(8,128)(2,1)S(1)} custom-call(s32[1]{0:T(128)} %bitcast.me_ref, s32[4]{0:T(128)S(1)} %copy-done.4, s32[32]{0:T(128)S(1)} %copy-done.6, s32[4]{0:T(128)S(1)} %copy-done.8, bf16[8,256,256]{2,1,0:T(8,128)(2,1)S(1)} %constant_dynamic-update-slice_fusion.2.refs_0_, bf16[8,256,256]{2,1,0:T(8,128)(2,1)S(1)} %collective-permute-done.4.refs_1_, ...), custom_call_target="tpu_custom_call" | custom-call | bytes 2097152 | tf_op jit(solution)/shard_map/pick_home/pallas_call | solution.py:56
  98.8 2.6 %collective-permute-done.8.refs_4_ = bf16[8,256,256]{2,1,0:T(8,128)(2,1)S(1)} collective-permute-done((bf16[8,256,256]{2,1,0:T(8,128)(2,1)S(1)}, bf16[8,256,256]{2,1,0:T(8,128)(2,1)S(1)}, u32[]{:S(2)}, u32[]{:S(2)}) %collective-permute-start.8) | collective-permute-done | bytes 1048608 | tf_op jit(solution)/shard_map/ppermute | solution.py:266
  101.4 1.2 copy-done.2
  102.6 2.3 %place_cache.1 = (bf16[4096,128]{1,0:T(8,128)(2,1)}, bf16[4096,128]{1,0:T(8,128)(2,1)}) custom-call(s32[1]{0:T(128)} %bitcast.me_ref, s32[4]{0:T(128)S(1)} %copy-done.4, s32[32]{0:T(128)S(1)} %copy-done.6, s32[4]{0:T(128)S(1)} %copy-done.8, bf16[8,256,256]{2,1,0:T(8,128)(2,1)S(1)} %constant_dynamic-update-slice_fusion.2.refs_0_, ...), custom_call_target="tpu_custom_call" | custom-call | bytes 4194304 | tf_op jit(solution)/shard_map/place_cache/pallas_call | solution.py:234
  105.0 43.9 %reduce-scatter.2.cloned.1.call-done = bf16[64,4096]{1,0:T(8,128)(2,1)} async-done(((bf16[512,4096]{1,0:T(8,128)(2,1)}), bf16[64,4096]{1,0:T(8,128)(2,1)}) %reduce-scatter.2.cloned.1.call-update) | async-done | bytes 524304 | tf_op jit(solution)/shard_map/reduce_scatter | solution.py:285
  (32 shorter events, 4.6 us)
Async XLA Ops:
  7.2 54.1 %copy-start.4 = (s32[4]{0:T(128)S(1)}, s32[4]{0:T(128)}, u32[]{:S(2)}) copy-start(s32[4]{0:T(128)} %lengths.7) | copy-start | bytes 52
  7.2 54.1 %copy-start.6 = (s32[32]{0:T(128)S(1)}, s32[32]{0:T(128)}, u32[]{:S(2)}) copy-start(s32[32]{0:T(128)} %stretch_owner.7) | copy-start | bytes 388
  7.2 141.7 %reduce-scatter.2.cloned.1.call-start = ((), (), s32[]{:S(2)}) async-start(), calls=%async_computation.1 | async-start | bytes 4718592 | tf_op jit(solution)/shard_map/reduce_scatter | solution.py:285
  9.2 1.7 %collective-permute-start = (bf16[256,256]{1,0:T(8,128)(2,1)S(1)}, bf16[256,256]{1,0:T(8,128)(2,1)S(1)}, u32[]{:S(2)}, u32[]{:S(2)}) collective-permute-start(bf16[256,256]{1,0:T(8,128)(2,1)S(1)} %constant_dynamic-slice_fusion), channel_id=1, source_target_pairs={{0,8},{8,0},{16,24},{24,16},{32,40},{40,32},{48,56},{56,48},{64,72... | collective-permute-start | bytes 393224 | tf_op jit(solution)/shard_map/ppermute | solution.py:266
  10.9 8.9 %collective-permute-start.1 = (bf16[2,256,256]{2,1,0:T(8,128)(2,1)S(1)}, bf16[2,256,256]{2,1,0:T(8,128)(2,1)S(1)}, u32[]{:S(2)}, u32[]{:S(2)}) collective-permute-start(bf16[2,256,256]{2,1,0:T(8,128)(2,1)S(1)} %pad_maximum_fusion), channel_id=1, source_target_pairs={{64,0},{24,8},{80,16},{40,24},{96,32},{56,40},{112,48},{8,56},{128... | collective-permute-start | bytes 786440 | tf_op jit(solution)/shard_map/ppermute | solution.py:275
  13.8 6.8 %collective-permute-start.2 = (bf16[2,256,256]{2,1,0:T(8,128)(2,1)S(1)}, bf16[2,256,256]{2,1,0:T(8,128)(2,1)S(1)}, u32[]{:S(2)}, u32[]{:S(2)}) collective-permute-start(bf16[2,256,256]{2,1,0:T(8,128)(2,1)S(1)} %pad_maximum_fusion), channel_id=1, source_target_pairs={{128,0},{40,8},{144,16},{56,24},{160,32},{8,40},{176,48},{24,56},{... | collective-permute-start | bytes 786440 | tf_op jit(solution)/shard_map/ppermute | solution.py:275
  14.1 9.2 %collective-permute-start.3 = (bf16[2,256,256]{2,1,0:T(8,128)(2,1)S(1)}, bf16[2,256,256]{2,1,0:T(8,128)(2,1)S(1)}, u32[]{:S(2)}, u32[]{:S(2)}) collective-permute-start(bf16[2,256,256]{2,1,0:T(8,128)(2,1)S(1)} %pad_maximum_fusion), channel_id=1, source_target_pairs={{192,0},{56,8},{208,16},{8,24},{224,32},{24,40},{240,48},{40,56},{... | collective-permute-start | bytes 786440 | tf_op jit(solution)/shard_map/ppermute | solution.py:275
  23.3 14.0 %collective-permute-start.4 = (bf16[8,256,256]{2,1,0:T(8,128)(2,1)S(1)}, bf16[8,256,256]{2,1,0:T(8,128)(2,1)S(1)}, u32[]{:S(2)}, u32[]{:S(2)}) collective-permute-start(bf16[8,256,256]{2,1,0:T(8,128)(2,1)S(1)} %constant_dynamic-update-slice_fusion.2.refs_0_), channel_id=1, source_target_pairs={{16,0},{72,8},{32,16},{88,24},{48,32},{104,40},{0,48},{120,56},{80... | collective-permute-start | bytes 3145736 | tf_op jit(solution)/shard_map/ppermute | solution.py:276
  23.9 25.6 %collective-permute-start.5 = (bf16[8,256,256]{2,1,0:T(8,128)(2,1)S(1)}, bf16[8,256,256]{2,1,0:T(8,128)(2,1)S(1)}, u32[]{:S(2)}, u32[]{:S(2)}) collective-permute-start(bf16[8,256,256]{2,1,0:T(8,128)(2,1)S(1)} %constant_dynamic-update-slice_fusion.2.refs_0_), channel_id=1, source_target_pairs={{32,0},{136,8},{48,16},{152,24},{0,32},{168,40},{16,48},{184,56},{... | collective-permute-start | bytes 3145736 | tf_op jit(solution)/shard_map/ppermute | solution.py:276
  25.8 24.6 %collective-permute-start.6 = (bf16[8,256,256]{2,1,0:T(8,128)(2,1)S(1)}, bf16[8,256,256]{2,1,0:T(8,128)(2,1)S(1)}, u32[]{:S(2)}, u32[]{:S(2)}) collective-permute-start(bf16[8,256,256]{2,1,0:T(8,128)(2,1)S(1)} %constant_dynamic-update-slice_fusion.2.refs_0_), channel_id=1, source_target_pairs={{48,0},{200,8},{0,16},{216,24},{16,32},{232,40},{32,48},{248,56},{... | collective-permute-start | bytes 3145736 | tf_op jit(solution)/shard_map/ppermute | solution.py:276
  50.4 9.9 %copy-start = (bf16[8,256,256]{2,1,0:T(8,128)(2,1)}, bf16[8,256,256]{2,1,0:T(8,128)(2,1)S(1)}, u32[]{:S(2)}) copy-start(bf16[8,256,256]{2,1,0:T(8,128)(2,1)S(1)} %collective-permute-done.6.refs_3_) | copy-start | bytes 3145732
  50.4 0.7 copy-start.3
  51.1 0.7 copy-start.5
  51.7 0.7 copy-start.7
  55.0 40.1 %copy-start.8 = (s32[4]{0:T(128)S(1)}, s32[4]{0:T(128)}, u32[]{:S(2)}) copy-start(s32[4]{0:T(128)} %home_replica.7) | copy-start | bytes 52
  55.0 5.3 %collective-permute-start.7 = (bf16[8,256,256]{2,1,0:T(8,128)(2,1)S(1)}, bf16[8,256,256]{2,1,0:T(8,128)(2,1)S(1)}, u32[]{:S(2)}, u32[]{:S(2)}) collective-permute-start(bf16[8,256,256]{2,1,0:T(8,128)(2,1)S(1)} %pick_visible.1), channel_id=1, source_target_pairs={{0,8},{8,0},{16,24},{24,16},{32,40},{40,32},{48,56},{56,48},{64,72... | collective-permute-start | bytes 3145736 | tf_op jit(solution)/shard_map/ppermute | solution.py:266
  60.3 1.0 copy-start.10
  61.3 1.2 copy-start.9
  95.1 1.2 copy-start.1
  98.7 2.7 %collective-permute-start.8 = (bf16[8,256,256]{2,1,0:T(8,128)(2,1)S(1)}, bf16[8,256,256]{2,1,0:T(8,128)(2,1)S(1)}, u32[]{:S(2)}, u32[]{:S(2)}) collective-permute-start(bf16[8,256,256]{2,1,0:T(8,128)(2,1)S(1)} %pick_home.1), channel_id=1, source_target_pairs={{0,8},{8,0},{16,24},{24,16},{32,40},{40,32},{48,56},{56,48},{64,72... | collective-permute-start | bytes 3145736 | tf_op jit(solution)/shard_map/ppermute | solution.py:266
  101.4 1.2 copy-start.2
Sparse Core Ops, SparseCore 0:
  95.2 53.6 reduce-scatter.1
